TPU v7x, 32 devices: a whole 2x2x4 slice. The times are simulated.
32 devices in a mesh: frame: 16 (over z, y, core), pix: 2 (over x).
Axes of the slice: x: 2, y: 2, z: 4, core: 2. Of those that a mesh axis runs over, the one named last changes fastest.
Arguments:
- library: float32 [6144, 3072], P('frame', 'pix'), may hold values from -5000 to 5000
- annulus: int32 [1536], P('pix'), may hold values from 0 to 1535, as said below
Outputs:
- gram: float32 [6144, 6144], P('frame', 'pix')
Inputs may be any that keep to these rules, and one draw needn't show every extreme that they name: `annulus`: within each aligned block of 768 entries the values are distinct and rising, and each block holds both 0 and 1535.
All inputs are finite; a program needn't handle non-finite values.
Results may differ from a plain program's by a relative error of at most 0.000065.
Values sent between devices are 32-bit elements; how exact they have to be, the bound alone decides.
No kernel may reach another device: no remote copies, remote signals or barrier semaphores. Data moves between devices by JAX's collectives and lax.ppermute only.
A program may use at most 128 MiB of HBM per device.

v0:
```python
import jax
import jax.numpy as jnp
from jax import lax
from jax.sharding import PartitionSpec as P

PIX = 1536


def local(library, annulus):
    picked = jnp.take(library, annulus, axis=1)
    total = lax.psum(jnp.sum(picked, axis=1), "pix")
    frame_mean = total / PIX
    centered = picked - frame_mean[:, None]
    squares = lax.psum(jnp.sum(centered * centered, axis=1), "pix")
    unit = centered / jnp.sqrt(squares + 1e-06)[:, None]
    partial_gram = lax.dot_general(
        unit,
        lax.all_gather(unit, "frame", axis=0, tiled=True),
        (((1,), (1,)), ((), ())),
        precision=lax.Precision.HIGHEST,
        preferred_element_type=jnp.float32,
    )
    return lax.psum_scatter(partial_gram, "pix", scatter_dimension=1, tiled=True)


def solution(mesh):
    placed = (P("frame", "pix"), P("pix"))
    return jax.shard_map(
        local, mesh=mesh, in_specs=placed, out_specs=P("frame", "pix"), check_vma=False
    )
```

profile of v0, /device:TPU:0, one launch (start us, length us, event | category | flops | bytes accessed | tf_op | source)
XLA Modules:
  0.0 270.9 jit_solution(11756231896228547355)
XLA Ops:
  6.5 0.0 all-gather.2.cloned.1.call-start
  6.5 0.7 compare_and_fusion
  7.2 0.7 compare_select_fusion
  7.9 2.0 copy.3
  10.0 2.1 gather_fusion
  12.1 0.2 select_reduce_fusion
  12.3 5.8 %psum.14 = f32[384]{0:T(512)S(1)} all-reduce(f32[384]{0:T(512)S(1)} %select_reduce_fusion), channel_id=1, replica_groups=mesh['frame'=16,'pix'=2] {'pix'}, use_global_device_ids=true, to_apply=%region_1.2 | all-reduce | flops 384 | bytes 3072 | tf_op jit(solution)/shard_map/psum | solution.py:11
  18.1 0.2 multiply_reduce_fusion
  18.4 4.9 %psum.15 = f32[384]{0:T(512)S(1)} all-reduce(f32[384]{0:T(512)S(1)} %multiply_reduce_fusion), channel_id=1, replica_groups=mesh['frame'=16,'pix'=2] {'pix'}, use_global_device_ids=true, to_apply=%region_3.4 | all-reduce | flops 384 | bytes 3072 | tf_op jit(solution)/shard_map/psum | solution.py:14
  23.3 1.2 fusion.1
  24.6 0.0 all-gather.2.cloned.1.call-update
  24.6 0.0 reduce-scatter.2.cloned.1.call-start
  24.6 100.8 %all-gather.2.cloned.1.call-done = f32[6144,768]{0,1:T(8,128)} async-done(((f32[384,768]{0,1:T(8,128)}), f32[6144,768]{0,1:T(8,128)}) %all-gather.2.cloned.1.call-update) | async-done | bytes 18874384 | tf_op jit(solution)/shard_map/all_gather | solution.py:18
  125.5 27.9 %fusion = f32[384,6144]{1,0:T(8,128)} fusion(f32[6144,768]{0,1:T(8,128)} %all-gather.2.cloned.1.call-done, f32[768,384]{1,0:T(8,128)S(1)} %gather_fusion, f32[384]{0:T(512)S(1)} %add_sqrt_fusion, f32[384]{0:T(512)S(1)} %broadcast_multiply_fusion, pred[768]{0:T(1024)(128)(4,1)S(1)} %compare_and_fusion), kind=kOutput, calls=%fused_computation.4 | convolution fusion | flops 21744156672 | bytes 29495040 | tf_op jit(solution)/shard_map/dot_general | solution.py:16
  153.3 0.0 reduce-scatter.2.cloned.1.call-update
  153.4 110.7 %reduce-scatter.2.cloned.1.call-done = f32[384,3072]{1,0:T(8,128)} async-done(((f32[384,6144]{1,0:T(8,128)}), f32[384,3072]{1,0:T(8,128)}) %reduce-scatter.2.cloned.1.call-update) | async-done | bytes 4718608 | tf_op jit(solution)/shard_map/reduce_scatter | solution.py:23
  (3 shorter events, 0.0 us)
Async XLA Ops:
  6.5 118.9 %all-gather.2.cloned.1.call-start = ((), (), s32[]{:S(2)}) async-start(), calls=%async_computation.1 | async-start | bytes 20054016 | tf_op jit(solution)/shard_map/all_gather | solution.py:18
  24.6 239.5 %reduce-scatter.2.cloned.1.call-start = ((), (), s32[]{:S(2)}) async-start(), calls=%async_computation.2 | async-start | bytes 14155776 | tf_op jit(solution)/shard_map/reduce_scatter | solution.py:23
Sparse Core Ops, SparseCore 0:
  24.7 100.7 all-gather.1
  153.5 110.5 reduce-scatter.1
where the time goes:
time: 271 us
  waiting for transfers between devices  212 us (78%)
  matrix products  27.9 us (10%)
  between operations  13.4 us (5%)
  blocking collectives  10.8 us (4%)
  local copies, waits for them, and re-layouts  4.17 us (2%)
  other arithmetic  3.06 us (1%)
    reduce_scatter x1, waiting for transfers between devices, local(): lax.psum_scatter(partial_gram, 'pix', scatter_dimension=1, tiled=True)  111 us
    all_gather x1, waiting for transfers between devices, local(): lax.all_gather(unit, 'frame', axis=0, tiled=True)  101 us
    dot_general x1, matrix products, local(): lax.dot_general(unit, lax.all_gather(unit, 'frame', axis=0, tiled=True),...  27.9 us
    psum x1, blocking collectives, local(): total = lax.psum(jnp.sum(picked, axis=1), 'pix')  5.84 us
  transfers between devices with their start and end apart: 2, of which 2 were waited for; matrix products, arithmetic and copies ran while one was open for 0% of the time, Pallas kernels for 0%

commit v1 on v0

v1 whole, which is shorter than its diff:
```python
import functools

import jax
import jax.numpy as jnp
from jax import lax
from jax.experimental import pallas as pl
from jax.experimental.pallas import tpu as pltpu
from jax.sharding import PartitionSpec as P

PIX = 1536
EPS = 1e-06
GROUPS = ((64, 64), (128,), (128,))
PIECES = tuple(rows for group in GROUPS for rows in group)
STAT_ROWS = 8
VMEM = 60 << 20
F32, BF16 = jnp.float32, jnp.bfloat16
NT = (((1,), (1,)), ((), ()))


def split(a):
    high = a.astype(BF16)
    return high, (a - high.astype(F32)).astype(BF16)


def dot_nt(high, low, b):
    b_high, b_low = split(b)
    dot = functools.partial(
        lax.dot_general, dimension_numbers=NT, preferred_element_type=F32
    )
    return dot(high, b_high) + (dot(high, b_low) + dot(low, b_high))


def pick_kernel(annulus_ref, library_ref, high_ref, low_ref, *piece_refs):
    rows, band = library_ref.shape
    pix = annulus_ref.shape[1]
    tile = 256
    width = band - pix + tile
    columns = []
    for start in range(0, pix, tile):
        a = library_ref[:, start : start + width]
        high, rest = split(a)
        mid, low = split(a - high.astype(F32))
        where = annulus_ref[:, start : start + tile] - start
        one_hot = jnp.where(
            lax.broadcasted_iota(jnp.int32, (width, tile), 0) == where, 1.0, 0.0
        ).astype(BF16)
        parts = jnp.dot(
            jnp.concatenate([high, mid, low], axis=0),
            one_hot,
            preferred_element_type=F32,
        )
        columns.append(
            parts[:rows] + parts[rows : 2 * rows] + parts[2 * rows :]
        )
    picked = jnp.concatenate(columns, axis=1)
    mean = jnp.sum(picked, axis=1, keepdims=True) / pix
    centered = picked - mean
    shift = jnp.sum(centered, axis=1, keepdims=True) / pix
    centered = centered - shift
    mean = mean + shift
    squares = jnp.sum(centered * centered, axis=1, keepdims=True)
    unit = centered / jnp.sqrt(squares + EPS)
    high_ref[...], low_ref[...] = split(unit)
    start = 0
    for ref, count in zip(piece_refs, PIECES):
        ref[:count] = unit[start : start + count]
        start += count
    first = piece_refs[0]
    count = PIECES[0]
    as_row = [
        jnp.transpose(jnp.broadcast_to(v, (rows, 128)))[:STAT_ROWS]
        for v in (mean, squares)
    ]
    first[count:] = jnp.concatenate(as_row, axis=1)


def pick(library, annulus):
    rows = library.shape[0]
    pix = annulus.shape[0]
    shapes = [jax.ShapeDtypeStruct((rows, pix), BF16)] * 2
    for i, count in enumerate(PIECES):
        shapes.append(
            jax.ShapeDtypeStruct((count + (STAT_ROWS if i == 0 else 0), pix), F32)
        )
    return pl.pallas_call(
        pick_kernel,
        out_shape=shapes,
        compiler_params=pltpu.CompilerParams(vmem_limit_bytes=VMEM),
        name="pick",
    )(annulus.reshape(1, pix), library)


def send_kernel(count, x_ref, high_ref, low_ref, gathered_ref, *refs):
    out_ref = refs[-1]
    b = gathered_ref[:, :count, :]
    b = b.reshape(-1, b.shape[-1])
    out_ref[0] = dot_nt(high_ref[...], low_ref[...], b)


def send_product(x, high, low, gathered, count, after):
    rows, pix = high.shape
    frames = gathered.shape[0]
    per = 256 // count
    steps = frames // 2 // per
    whole = lambda i, x: (0, 0)
    return pl.pallas_call(
        functools.partial(send_kernel, count),
        grid_spec=pltpu.PrefetchScalarGridSpec(
            num_scalar_prefetch=1,
            grid=(steps,),
            in_specs=[
                pl.BlockSpec((rows, pix), whole),
                pl.BlockSpec((rows, pix), whole),
                pl.BlockSpec(
                    (per, gathered.shape[1], pix),
                    lambda i, x: ((1 - x[0]) * steps + i, 0, 0),
                ),
            ]
            + [pl.BlockSpec(memory_space=pl.ANY)] * len(after),
            out_specs=pl.BlockSpec((1, rows, 256), lambda i, x: (i, 0, 0)),
        ),
        out_shape=jax.ShapeDtypeStruct((steps, rows, 256), F32),
        compiler_params=pltpu.CompilerParams(vmem_limit_bytes=VMEM),
        cost_estimate=pl.CostEstimate(
            flops=6 * rows * steps * 256 * pix,
            bytes_accessed=4 * steps * 256 * (pix + rows),
            transcendentals=0,
        ),
        name="send_product",
    )(x, high, low, gathered, *after)


def keep_kernel(group, index, x_ref, high_ref, low_ref, own_ref, stat_ref, *refs):
    n = len(group)
    gathered, received, out_ref = refs[:n], refs[n : 2 * n], refs[-1]
    b = [ref[0, :count, :] for ref, count in zip(gathered, group)]
    b = b[0] if n == 1 else jnp.concatenate(b, axis=0)
    kept = dot_nt(high_ref[...], low_ref[...], b)
    if n == 1:
        other = received[0][0]
    else:
        odd = lax.rem(pl.program_id(0), 2) == 1
        half = group[0]
        left = jnp.concatenate([ref[0][:, :half] for ref in received], axis=1)
        right = jnp.concatenate([ref[0][:, half:] for ref in received], axis=1)
        other = jnp.where(odd, right, left)
    at = slice(128 * index, 128 * index + 128)
    own, stat = own_ref[...], stat_ref[0]
    out_ref[...] = (
        own[:, 0:1] * stat[0:1, at] * kept
        + own[:, 1:2] * stat[1:2, at] * other
        + own[:, 2:3] * stat[2:3, at]
    )


def keep_product(x, high, low, own, stats, gathered, received, group, index, out):
    rows, pix = high.shape
    frames = gathered[0].shape[0] // 2
    whole = lambda i, x: (0, 0)
    in_specs = [
        pl.BlockSpec((rows, pix), whole),
        pl.BlockSpec((rows, pix), whole),
        pl.BlockSpec(own.shape, whole),
        pl.BlockSpec((1,) + stats.shape[1:], lambda i, x: (x[0] * frames + i, 0, 0)),
    ]
    for g in gathered:
        in_specs.append(
            pl.BlockSpec((1,) + g.shape[1:], lambda i, x: (x[0] * frames + i, 0, 0))
        )
    for count in group:
        if count == 128:
            at = lambda i, x: (i // 2, 0, lax.rem(i, 2))
        else:
            at = lambda i, x: (i // 4, 0, lax.rem(i // 2, 2))
        in_specs.append(pl.BlockSpec((1, rows, 128), at))
    operands = [x, high, low, own, stats, *gathered, *received]
    alias = {}
    if out is not None:
        in_specs.append(pl.BlockSpec(memory_space=pl.ANY))
        alias = {len(operands): 0}
        operands.append(out)
    return pl.pallas_call(
        functools.partial(keep_kernel, group, index),
        grid_spec=pltpu.PrefetchScalarGridSpec(
            num_scalar_prefetch=1,
            grid=(frames,),
            in_specs=in_specs,
            out_specs=pl.BlockSpec(
                (rows, 128), lambda i, x: (0, i * (rows // 128) + index)
            ),
        ),
        out_shape=jax.ShapeDtypeStruct((rows, frames * rows), F32),
        input_output_aliases=alias,
        compiler_params=pltpu.CompilerParams(vmem_limit_bytes=VMEM),
        cost_estimate=pl.CostEstimate(
            flops=6 * rows * frames * 128 * pix,
            bytes_accessed=4 * frames * 128 * (pix + 2 * rows),
            transcendentals=0,
        ),
        name="keep_product",
    )(*operands)


def scales(mine, other, frame, rows, pix):
    both = jnp.stack([mine, other])
    mean, squares = both[:, :, :rows], both[:, :, rows:]
    gap = (mean[0] - mean[1]) / 2
    total = squares[0] + squares[1] + (2 * pix) * (gap * gap)
    length = jnp.sqrt(total + EPS)
    part = jnp.sqrt(squares + EPS) / length
    stats = jnp.stack([part[0], part[1], (2 * pix) ** 0.5 * gap / length], axis=1)
    own = lax.dynamic_index_in_dim(stats, frame, 0, keepdims=False).T
    return jnp.pad(own, ((0, 0), (0, 125))), jnp.pad(stats, ((0, 0), (0, 5), (0, 0)))


def local_pair(library, annulus):
    rows = library.shape[0]
    pix = annulus.shape[0]
    swap = [(0, 1), (1, 0)]
    x = lax.axis_index("pix").astype(jnp.int32).reshape(1)
    high, low, *pieces = pick(library, annulus)
    gathered = [lax.all_gather(p, "frame", axis=0) for p in pieces]
    mine = gathered[0][:, PIECES[0], :]
    received, after = [], []
    for g, count in zip(gathered, PIECES):
        product = send_product(x, high, low, g, count, after)
        after = [product] + received[-1:]
        received.append(lax.ppermute(product, "pix", swap))
    other = lax.ppermute(mine, "pix", swap)
    own, stats = scales(mine, other, lax.axis_index("frame"), rows, pix)
    out, at = None, 0
    for index, group in enumerate(GROUPS):
        n = len(group)
        out = keep_product(
            x, high, low, own, stats,
            gathered[at : at + n], received[at : at + n], group, index, out,
        )
        at += n
    return out


def local(library, annulus):
    picked = jnp.take(library, annulus, axis=1)
    total = lax.psum(jnp.sum(picked, axis=1), "pix")
    frame_mean = total / PIX
    centered = picked - frame_mean[:, None]
    squares = lax.psum(jnp.sum(centered * centered, axis=1), "pix")
    unit = centered / jnp.sqrt(squares + EPS)[:, None]
    partial_gram = lax.dot_general(
        unit,
        lax.all_gather(unit, "frame", axis=0, tiled=True),
        (((1,), (1,)), ((), ())),
        precision=lax.Precision.HIGHEST,
        preferred_element_type=jnp.float32,
    )
    return lax.psum_scatter(partial_gram, "pix", scatter_dimension=1, tiled=True)


def solution(mesh):
    placed = (P("frame", "pix"), P("pix"))
    pair = mesh.shape["pix"] == 2 and mesh.shape["frame"] % 8 == 0
    return jax.shard_map(
        local_pair if pair else local,
        mesh=mesh, in_specs=placed, out_specs=P("frame", "pix"), check_vma=False,
    )
```

time: 271 us -> 318 us (1.17)
  Pallas kernels: 0 us -> 52 us
  matrix products: 27.9 us -> 0 us
  waiting for transfers between devices: 212 us -> 239 us
  blocking collectives: 10.8 us -> 0 us
  starting transfers between devices: 0.04 us -> 6.62 us
    reduce_scatter x1 -> x0, waiting for transfers between devices: 111 us -> none  [local(): lax.psum_scatter(partial_gram, 'pix', scatter_dimension=1, tiled=True)]
    all_gather x1 -> x4, waiting for transfers between devices: 101 us -> 203 us  [local_pair(): gathered = [lax.all_gather(p, 'frame', axis=0) for p in pieces]]
    pallas_call x0 -> x8, Pallas kernels: none -> 52 us  [the longest x3 28 us: keep_product(): pl.pallas_call(functools.partial(keep_kernel, group, index), grid_spec=pl...]
    ppermute x0 -> x5, waiting for transfers between devices: none -> 34.7 us  [the longest x1 34.7 us: local_pair(): other = lax.ppermute(mine, 'pix', swap)]
    dot_general x1 -> x0, matrix products: 27.9 us -> none  [local(): lax.dot_general(unit, lax.all_gather(unit, 'frame', axis=0, tiled=True),...]
    psum x2 -> x0, blocking collectives: 10.8 us -> none  [the longest x1 5.84 us: local(): total = lax.psum(jnp.sum(picked, axis=1), 'pix')]
    ppermute x0 -> x5, starting transfers between devices: none -> 6.5 us  [the longest x4 5.87 us: local_pair(): received.append(lax.ppermute(product, 'pix', swap))]
  transfers between devices with their start and end apart: 2 -> 9, of which waited for: 2 -> 5; matrix products, arithmetic and copies ran while one was open for 0% -> 1% of each run, Pallas kernels for 0% -> 12%
where the time goes in v1:
time: 318 us; the launch traced here: 317 us
  waiting for transfers between devices  239 us (75%)
  Pallas kernels  52 us (16%)
  between operations  13.2 us (4%)
  starting transfers between devices  6.62 us (2%)
  local copies, waits for them, and re-layouts  5.04 us (2%)
    all_gather x4, waiting for transfers between devices, local_pair(): gathered = [lax.all_gather(p, 'frame', axis=0) for p in pieces]  203 us
    ppermute x1, waiting for transfers between devices, local_pair(): other = lax.ppermute(mine, 'pix', swap)  34.7 us
    pallas_call x3, Pallas kernels, keep_product(): pl.pallas_call(functools.partial(keep_kernel, group, index), grid_spec=pl...  28 us
    pallas_call x4, Pallas kernels, send_product(): pl.pallas_call(functools.partial(send_kernel, count), grid_spec=pltpu.Pre...  18.5 us
  transfers between devices with their start and end apart: 9, of which 5 were waited for; matrix products, arithmetic and copies ran while one was open for 1% of the time, Pallas kernels for 12%

profile of v1, /device:TPU:0, one launch (start us, length us, event | category | flops | bytes accessed | tf_op | source)
XLA Modules:
  0.0 316.6 jit_solution(18134321032383368413)
XLA Ops:
  6.5 0.0 all-gather.9.cloned.1.call-start
  6.5 1.2 reshape.74.annulus_ref
  7.8 5.5 %pick.1 = (bf16[384,768]{1,0:T(8,128)(2,1)}, bf16[384,768]{1,0:T(8,128)(2,1)}, f32[72,768]{1,0:T(8,128)}, f32[64,768]{1,0:T(8,128)}, f32[128,768]{1,0:T(8,128)}, /*index=5*/f32[128,768]{1,0:T(8,128)}) custom-call(s32[1,768]{1,0:T(1,128)} %reshape.74.annulus_ref, f32[384,1536]{1,0:T(8,128)} %library_ref.1), custom_call_target="tpu_custom_call" | custom-call | tf_op jit(solution)/shard_map/pick/pallas_call | solution.py:85
  13.2 0.0 all-gather.9.cloned.1.call-update
  13.3 0.0 all-gather.15.cloned.1.call-start
  13.3 0.7 all-gather.15.cloned.1.call-update
  14.0 0.0 all-gather.13.cloned.1.call-start
  14.1 0.7 all-gather.13.cloned.1.call-update
  14.8 0.0 all-gather.11.cloned.1.call-start
  14.8 0.5 all-gather.11.cloned.1.call-update
  15.3 48.0 %all-gather.9.cloned.1.call-done = f32[1152,768]{1,0:T(8,128)} async-done(((f32[72,768]{1,0:T(8,128)}), f32[1152,768]{1,0:T(8,128)}) %all-gather.9.cloned.1.call-update) | async-done | bytes 3538960 | tf_op jit(solution)/shard_map/all_gather | solution.py:222
  63.3 3.6 %send_product.4.refs_0_ = f32[2,384,256]{2,1,0:T(8,128)} custom-call(s32[1]{0:T(128)} %bitcast.x_ref, bf16[384,768]{1,0:T(8,128)(2,1)} %get-tuple-element.11.high_ref, bf16[384,768]{1,0:T(8,128)(2,1)} %get-tuple-element.12.low_ref, f32[16,72,768]{2,1,0:T(8,128)} %bitcast.26), custom_call_target="tpu_custom_call" | custom-call | flops 905969664 | bytes 2359296 | tf_op jit(solution)/shard_map/send_product/pallas_call | solution.py:106
  66.9 1.5 collective-permute-start.1
  68.4 41.4 %all-gather.15.cloned.1.call-done = f32[1024,768]{1,0:T(8,128)} async-done(((f32[64,768]{1,0:T(8,128)}), f32[1024,768]{1,0:T(8,128)}) %all-gather.15.cloned.1.call-update) | async-done | bytes 3145744 | tf_op jit(solution)/shard_map/all_gather | solution.py:222
  109.8 3.6 %send_product.5.refs_0_ = f32[2,384,256]{2,1,0:T(8,128)} custom-call(s32[1]{0:T(128)} %bitcast.x_ref, bf16[384,768]{1,0:T(8,128)(2,1)} %get-tuple-element.11.high_ref, bf16[384,768]{1,0:T(8,128)(2,1)} %get-tuple-element.12.low_ref, f32[16,64,768]{2,1,0:T(8,128)} %bitcast.29, f32[2,384,256]{2,1,0:T(8,128)} %send_product.4.refs_0_), custom_call_target="tpu_custom_call" | custom-call | flops 905969664 | bytes 2359296 | tf_op jit(solution)/shard_map/send_product/pallas_call | solution.py:106
  113.4 1.5 collective-permute-start.2
  114.9 0.0 collective-permute-done.1.refs_1_.refs_2_
  114.9 0.0 copy-start.1
  114.9 57.9 %all-gather.13.cloned.1.call-done = f32[2048,768]{1,0:T(8,128)} async-done(((f32[128,768]{1,0:T(8,128)}), f32[2048,768]{1,0:T(8,128)}) %all-gather.13.cloned.1.call-update) | async-done | bytes 6291472 | tf_op jit(solution)/shard_map/all_gather | solution.py:222
  172.8 0.0 copy-done.1
  172.8 5.6 %send_product.6.refs_0_ = f32[4,384,256]{2,1,0:T(8,128)} custom-call(s32[1]{0:T(128)} %bitcast.x_ref, bf16[384,768]{1,0:T(8,128)(2,1)} %get-tuple-element.11.high_ref, bf16[384,768]{1,0:T(8,128)(2,1)} %get-tuple-element.12.low_ref, f32[16,128,768]{2,1,0:T(8,128)} %bitcast.24, f32[2,384,256]{2,1,0:T(8,128)} %send_product.5.refs_0_, f32[2,384,256]{2,1,0:T(8,128)} %copy-done.1), custom_call_target="tpu_custom_call" | custom-call | flops 1811939328 | bytes 4718592 | tf_op jit(solution)/shard_map/send_product/pallas_call | solution.py:106
  178.4 1.5 collective-permute-start.4
  179.9 0.0 collective-permute-done.2.refs_1_.refs_3_
  179.9 0.0 copy-start
  179.9 55.5 %all-gather.11.cloned.1.call-done = f32[2048,768]{1,0:T(8,128)} async-done(((f32[128,768]{1,0:T(8,128)}), f32[2048,768]{1,0:T(8,128)}) %all-gather.11.cloned.1.call-update) | async-done | bytes 6291472 | tf_op jit(solution)/shard_map/all_gather | solution.py:222
  235.4 0.0 copy-done
  235.4 5.6 %send_product.7 = f32[4,384,256]{2,1,0:T(8,128)} custom-call(s32[1]{0:T(128)} %bitcast.x_ref, bf16[384,768]{1,0:T(8,128)(2,1)} %get-tuple-element.11.high_ref, bf16[384,768]{1,0:T(8,128)(2,1)} %get-tuple-element.12.low_ref, f32[16,128,768]{2,1,0:T(8,128)} %bitcast.22, f32[4,384,256]{2,1,0:T(8,128)} %send_product.6.refs_0_, f32[2,384,256]{2,1,0:T(8,128)} %copy-done), custom_call_target="tpu_custom_call" | custom-call | flops 1811939328 | bytes 4718592 | tf_op jit(solution)/shard_map/send_product/pallas_call | solution.py:106
  241.1 1.5 collective-permute-start.3
  242.5 1.0 slice_bitcast_fusion.2
  243.6 0.6 collective-permute-start
  244.2 34.7 %collective-permute-done = f32[16,768]{1,0:T(8,128)S(1)} collective-permute-done((f32[16,768]{1,0:T(8,128)S(1)}, f32[16,768]{1,0:T(8,128)S(1)}, u32[]{:S(2)}, u32[]{:S(2)}) %collective-permute-start) | collective-permute-done | bytes 49184 | tf_op jit(solution)/shard_map/ppermute | solution.py:229
  278.9 0.1 fusion.5
  279.0 0.1 fusion.2
  279.2 0.1 slice_bitcast_fusion.1
  279.2 0.1 pad_maximum_fusion
  279.3 0.1 copy.5
  279.5 0.7 pad.9.stat_ref
  280.2 0.7 pad.8.own_ref
  280.9 9.8 %keep_product.3.refs_2_ = f32[384,3072]{1,0:T(8,128)} custom-call(s32[1]{0:T(128)} %bitcast.x_ref, bf16[384,768]{1,0:T(8,128)(2,1)} %get-tuple-element.11.high_ref, bf16[384,768]{1,0:T(8,128)(2,1)} %get-tuple-element.12.low_ref, f32[384,128]{1,0:T(8,128)} %pad.8.own_ref, f32[16,8,384]{2,1,0:T(8,128)} %pad.9.stat_ref, f32[16,72,768]{2,1,0:T(8,128)} %bitcast.28, ...), custom_call_target="tpu_custom_call" | custom-call | flops 1811939328 | bytes 6291456 | tf_op jit(solution)/shard_map/keep_product/pallas_call | solution.py:182
  290.6 0.0 collective-permute-done.4.refs_1_
  290.6 0.0 copy-start.2
  290.6 1.2 copy-done.2
  291.8 9.1 %keep_product.4.refs_2_ = f32[384,3072]{1,0:T(8,128)} custom-call(s32[1]{0:T(128)} %bitcast.x_ref, bf16[384,768]{1,0:T(8,128)(2,1)} %get-tuple-element.11.high_ref, bf16[384,768]{1,0:T(8,128)(2,1)} %get-tuple-element.12.low_ref, f32[384,128]{1,0:T(8,128)} %pad.8.own_ref, f32[16,8,384]{2,1,0:T(8,128)} %pad.9.stat_ref, ...), custom_call_target="tpu_custom_call", output_to_operand_aliasing={{}: (7, {})} | custom-call | flops 1811939328 | bytes 6291456 | tf_op jit(solution)/shard_map/keep_product/pallas_call | solution.py:182
  300.9 0.0 collective-permute-done.3.refs_1_
  301.0 9.2 %keep_product.5 = f32[384,3072]{1,0:T(8,128)} custom-call(s32[1]{0:T(128)} %bitcast.x_ref, bf16[384,768]{1,0:T(8,128)(2,1)} %get-tuple-element.11.high_ref, bf16[384,768]{1,0:T(8,128)(2,1)} %get-tuple-element.12.low_ref, f32[384,128]{1,0:T(8,128)} %pad.8.own_ref, f32[16,8,384]{2,1,0:T(8,128)} %pad.9.stat_ref, ...), custom_call_target="tpu_custom_call", output_to_operand_aliasing={{}: (7, {})} | custom-call | flops 1811939328 | bytes 6291456 | tf_op jit(solution)/shard_map/keep_product/pallas_call | solution.py:182
  (4 shorter events, 0.1 us)
Async XLA Ops:
  6.5 56.8 %all-gather.9.cloned.1.call-start = ((), (), s32[]{:S(2)}) async-start(), calls=%async_computation | async-start | bytes 3760128 | tf_op jit(solution)/shard_map/all_gather | solution.py:222
  13.3 96.6 %all-gather.15.cloned.1.call-start = ((), (), s32[]{:S(2)}) async-start(), calls=%async_computation.3 | async-start | bytes 3342336 | tf_op jit(solution)/shard_map/all_gather | solution.py:222
  14.0 158.8 %all-gather.13.cloned.1.call-start = ((), (), s32[]{:S(2)}) async-start(), calls=%async_computation.2 | async-start | bytes 6684672 | tf_op jit(solution)/shard_map/all_gather | solution.py:222
  14.8 220.7 %all-gather.11.cloned.1.call-start = ((), (), s32[]{:S(2)}) async-start(), calls=%async_computation.1 | async-start | bytes 6684672 | tf_op jit(solution)/shard_map/all_gather | solution.py:222
  66.9 48.0 %collective-permute-start.1 = (f32[2,384,256]{2,1,0:T(8,128)}, f32[2,384,256]{2,1,0:T(8,128)S(1)}, u32[]{:S(2)}, u32[]{:S(2)}) collective-permute-start(f32[2,384,256]{2,1,0:T(8,128)} %send_product.4.refs_0_), channel_id=1, source_target_pairs={{0,1},{1,0},{2,3},{3,2},{4,5},{5,4},{6,7},{7,6},{8,9},{9,8},{10,11... | collective-permute-start | bytes 2359304 | tf_op jit(solution)/shard_map/ppermute | solution.py:228
  113.4 66.5 %collective-permute-start.2 = (f32[2,384,256]{2,1,0:T(8,128)}, f32[2,384,256]{2,1,0:T(8,128)S(1)}, u32[]{:S(2)}, u32[]{:S(2)}) collective-permute-start(f32[2,384,256]{2,1,0:T(8,128)} %send_product.5.refs_0_), channel_id=1, source_target_pairs={{0,1},{1,0},{2,3},{3,2},{4,5},{5,4},{6,7},{7,6},{8,9},{9,8},{10,11... | collective-permute-start | bytes 2359304 | tf_op jit(solution)/shard_map/ppermute | solution.py:228
  114.9 57.9 %copy-start.1 = (f32[2,384,256]{2,1,0:T(8,128)}, f32[2,384,256]{2,1,0:T(8,128)S(1)}, u32[]{:S(2)}) copy-start(f32[2,384,256]{2,1,0:T(8,128)S(1)} %collective-permute-done.1.refs_1_.refs_2_) | copy-start | bytes 2359300
  178.4 112.2 %collective-permute-start.4 = (f32[4,384,256]{2,1,0:T(8,128)}, f32[4,384,256]{2,1,0:T(8,128)S(1)}, u32[]{:S(2)}, u32[]{:S(2)}) collective-permute-start(f32[4,384,256]{2,1,0:T(8,128)} %send_product.6.refs_0_), channel_id=1, source_target_pairs={{0,1},{1,0},{2,3},{3,2},{4,5},{5,4},{6,7},{7,6},{8,9},{9,8},{10,11... | collective-permute-start | bytes 4718600 | tf_op jit(solution)/shard_map/ppermute | solution.py:228
  179.9 55.5 %copy-start = (f32[2,384,256]{2,1,0:T(8,128)}, f32[2,384,256]{2,1,0:T(8,128)S(1)}, u32[]{:S(2)}) copy-start(f32[2,384,256]{2,1,0:T(8,128)S(1)} %collective-permute-done.2.refs_1_.refs_3_) | copy-start | bytes 2359300
  241.1 59.9 %collective-permute-start.3 = (f32[4,384,256]{2,1,0:T(8,128)}, f32[4,384,256]{2,1,0:T(8,128)}, u32[]{:S(2)}, u32[]{:S(2)}) collective-permute-start(f32[4,384,256]{2,1,0:T(8,128)} %send_product.7), channel_id=1, source_target_pairs={{0,1},{1,0},{2,3},{3,2},{4,5},{5,4},{6,7},{7,6},{8,9},{9,8},{10,11... | collective-permute-start | bytes 4718600 | tf_op jit(solution)/shard_map/ppermute | solution.py:228
  243.6 35.3 %collective-permute-start = (f32[16,768]{1,0:T(8,128)S(1)}, f32[16,768]{1,0:T(8,128)S(1)}, u32[]{:S(2)}, u32[]{:S(2)}) collective-permute-start(f32[16,768]{1,0:T(8,128)S(1)} %bitcast.33), channel_id=1, source_target_pairs={{0,1},{1,0},{2,3},{3,2},{4,5},{5,4},{6,7},{7,6},{8,9},{9,8},{10,11... | collective-permute-start | bytes 147464 | tf_op jit(solution)/shard_map/ppermute | solution.py:229
  290.6 1.2 copy-start.2
Sparse Core Ops, SparseCore 0:
  13.4 49.8 all-gather.8
  65.6 44.1 all-gather.14
  112.1 60.6 all-gather.12
  174.9 60.4 all-gather.10

commit v2 on v0

v2 whole, which is shorter than its diff:
```python
import functools

import jax
import jax.numpy as jnp
from jax import lax
from jax.experimental import pallas as pl
from jax.experimental.pallas import tpu as pltpu
from jax.sharding import PartitionSpec as P

PIX = 1536
EPS = 1e-06
STEP = 128
STAT_ROWS = 8
VMEM = 56 << 20
F32, BF16 = jnp.float32, jnp.bfloat16


def split(a):
    high = a.astype(BF16)
    return high, (a - high.astype(F32)).astype(BF16)


def pick_kernel(annulus_ref, library_ref, centered_ref, stat_ref):
    rows, band = library_ref.shape
    pix = annulus_ref.shape[1]
    tile = 256
    width = band - pix + tile
    columns = []
    for start in range(0, pix, tile):
        a = library_ref[:, start : start + width]
        high, rest = split(a)
        mid, low = split(a - high.astype(F32))
        where = annulus_ref[:, start : start + tile] - start
        one_hot = jnp.where(
            lax.broadcasted_iota(jnp.int32, (width, tile), 0) == where, 1.0, 0.0
        ).astype(BF16)
        parts = jnp.dot(
            jnp.concatenate([high, mid, low], axis=0),
            one_hot,
            preferred_element_type=F32,
        )
        columns.append(
            parts[:rows] + parts[rows : 2 * rows] + parts[2 * rows :]
        )
    picked = jnp.concatenate(columns, axis=1)
    mean = jnp.sum(picked, axis=1, keepdims=True) / pix
    centered = picked - mean
    shift = jnp.sum(centered, axis=1, keepdims=True) / pix
    centered = centered - shift
    mean = mean + shift
    squares = jnp.sum(centered * centered, axis=1, keepdims=True)
    centered_ref[...] = centered
    as_row = [
        jnp.transpose(jnp.broadcast_to(v, (rows, 128)))[:STAT_ROWS]
        for v in (mean, squares)
    ]
    stat_ref[...] = jnp.concatenate(as_row, axis=1)


def pick(library, annulus):
    rows = library.shape[0]
    pix = annulus.shape[0]
    return pl.pallas_call(
        pick_kernel,
        out_shape=[
            jax.ShapeDtypeStruct((rows, pix), F32),
            jax.ShapeDtypeStruct((STAT_ROWS, 2 * rows), F32),
        ],
        compiler_params=pltpu.CompilerParams(vmem_limit_bytes=VMEM),
        name="pick",
    )(annulus.reshape(1, pix), library)


def unit_kernel(centered_ref, mine_ref, other_ref, unit_ref, *piece_refs):
    rows, pix = centered_ref.shape
    mine, other = mine_ref[0:1], other_ref[0:1]
    gap = (mine[:, :rows] - other[:, :rows]) / 2
    squares = mine[:, rows:] + other[:, rows:] + (2 * pix) * (gap * gap)
    length = jnp.sqrt(squares + EPS)
    gap, length = [
        jnp.transpose(jnp.broadcast_to(v, (128, rows)))[:, :1] for v in (gap, length)
    ]
    unit = (centered_ref[...] + gap) / length
    unit_ref[...] = unit
    for k, ref in enumerate(piece_refs):
        ref[...] = unit[k * STEP : (k + 1) * STEP]


def units(centered, mine, other):
    rows, pix = centered.shape
    return pl.pallas_call(
        unit_kernel,
        out_shape=[jax.ShapeDtypeStruct((rows, pix), F32)]
        + [jax.ShapeDtypeStruct((STEP, pix), F32)] * (rows // STEP),
        compiler_params=pltpu.CompilerParams(vmem_limit_bytes=VMEM),
        name="unit",
    )(centered, mine, other)


def rows_kernel(a_ref, b_ref, high_ref, low_ref):
    pix = a_ref.shape[1]
    high_ref[:, :pix], low_ref[:, :pix] = split(a_ref[...])
    high_ref[:, pix:], low_ref[:, pix:] = split(b_ref[...])


def split_rows(a, b):
    rows, pix = a.shape
    return pl.pallas_call(
        rows_kernel,
        out_shape=[jax.ShapeDtypeStruct((rows, 2 * pix), BF16)] * 2,
        compiler_params=pltpu.CompilerParams(vmem_limit_bytes=VMEM),
        cost_estimate=pl.CostEstimate(
            flops=6 * rows * pix, bytes_accessed=16 * rows * pix, transcendentals=0
        ),
        name="split_rows",
    )(a, b)


def product_kernel(n, choice_ref, *refs):
    row_refs, refs = refs[: 2 * n], refs[2 * n :]
    column_refs, out_ref = refs[:6], refs[6]
    here, there = [], []
    for j in range(2):
        near, far, received = column_refs[3 * j : 3 * j + 3]
        here.append(jnp.where(choice_ref[j] == 1, near[...], far[...]))
        there.append(received[...])
    columns = jnp.concatenate(
        [jnp.concatenate(here, axis=0), jnp.concatenate(there, axis=0)], axis=1
    )
    high, low = split(jnp.transpose(columns))
    for i in range(n):
        a_high, a_low = row_refs[2 * i][...], row_refs[2 * i + 1][...]
        rows = a_high.shape[0]
        both = jnp.dot(
            jnp.concatenate([a_high, a_low], axis=0), high, preferred_element_type=F32
        )
        cross = jnp.dot(a_high, low, preferred_element_type=F32)
        out_ref[i] = both[:rows] + (both[rows:] + cross)


def product(choice, rows, columns):
    n = len(rows) // 2
    count, depth = rows[0].shape
    vmem = pl.BlockSpec(memory_space=pltpu.VMEM)
    return pl.pallas_call(
        functools.partial(product_kernel, n),
        in_specs=[pl.BlockSpec(memory_space=pltpu.SMEM)]
        + [vmem] * (len(rows) + len(columns)),
        out_specs=vmem,
        out_shape=jax.ShapeDtypeStruct((n, count, 2 * STEP), F32),
        compiler_params=pltpu.CompilerParams(vmem_limit_bytes=VMEM),
        cost_estimate=pl.CostEstimate(
            flops=6 * n * count * 2 * STEP * depth,
            bytes_accessed=4 * n * count * depth + 4 * n * count * 2 * STEP,
            transcendentals=0,
        ),
        name="product",
    )(choice, *rows, *columns)


def place_kernel(at_ref, own_ref, y_ref, core_ref, both_ref, *refs):
    out_ref = refs[-1]
    source = lax.rem(pl.program_id(0), 4)
    for s, ref in enumerate((own_ref, core_ref, y_ref, both_ref)):

        @pl.when(source == s)
        def _():
            out_ref[...] = ref[0]


def place(at, own, from_y, from_core, from_both, frames, out):
    rows = own.shape[1]
    block = pl.BlockSpec((1, rows, STEP), lambda i, at: (0, 0, i // 4))
    operands = [at, own, from_y, from_core, from_both]
    in_specs = [block] * 4
    alias = {}
    if out is not None:
        in_specs.append(pl.BlockSpec(memory_space=pl.ANY))
        alias = {len(operands): 0}
        operands.append(out)
    return pl.pallas_call(
        place_kernel,
        grid_spec=pltpu.PrefetchScalarGridSpec(
            num_scalar_prefetch=1,
            grid=(8,),
            in_specs=in_specs,
            out_specs=pl.BlockSpec((rows, STEP), lambda i, at: (0, at[i])),
        ),
        out_shape=jax.ShapeDtypeStruct((rows, frames * rows), F32),
        input_output_aliases=alias,
        compiler_params=pltpu.CompilerParams(vmem_limit_bytes=VMEM),
        cost_estimate=pl.CostEstimate(
            flops=0, bytes_accessed=8 * rows * STEP * 8, transcendentals=0
        ),
        name="place",
    )(*operands)


def local_pair(library, annulus):
    rows = library.shape[0]
    frames = lax.axis_size("frame")
    frame = lax.axis_index("frame")
    x = lax.axis_index("pix")
    z = frame // 4

    def swap_x(a):
        return lax.ppermute(a, "pix", [(0, 1), (1, 0)])

    def swap_y(a):
        return lax.ppermute(a, "frame", [(f, f ^ 2) for f in range(frames)])

    def swap_core(a):
        return lax.ppermute(a, "frame", [(f, f ^ 1) for f in range(frames)])

    def next_z(a):
        return lax.ppermute(a, "frame", [(f, (f + 4) % frames) for f in range(frames)])

    centered, stat = pick(library, annulus)
    unit, *pieces = units(centered, stat, swap_x(stat))

    ring = [[p] for p in pieces]
    for _ in range(3):
        for blocks in ring:
            blocks.append(next_z(blocks[-1]))

    unit_x = swap_x(unit)
    mine = [unit, unit_x]
    far = [swap_y(a) for a in mine]
    near_rows = split_rows(*mine) + split_rows(*[swap_core(a) for a in mine])
    far_rows = split_rows(*far) + split_rows(*[swap_core(a) for a in far])

    choice = jnp.stack([((z - j) % 4) // 2 == x for j in range(2)]).astype(jnp.int32)
    places = jnp.stack(
        [
            (((z - j) % 2) * 4 + ((frame % 4) ^ s)) * (rows // STEP)
            for j in range(2)
            for s in range(4)
        ]
    ).astype(jnp.int32)
    out = None
    for k, blocks in enumerate(ring):
        columns = []
        for j in range(2):
            send = jnp.where(choice[j] == 1, blocks[j + 2], blocks[j])
            columns += [blocks[j], blocks[j + 2], swap_x(send)]
        near = product(choice, near_rows, columns)
        far = swap_y(product(choice, far_rows, columns))
        from_core = swap_core(near[1:])
        from_both = swap_core(far[1:])
        out = place(places + k, near, far, from_core, from_both, frames // 2, out)
    return out


def local(library, annulus):
    picked = jnp.take(library, annulus, axis=1)
    total = lax.psum(jnp.sum(picked, axis=1), "pix")
    frame_mean = total / PIX
    centered = picked - frame_mean[:, None]
    squares = lax.psum(jnp.sum(centered * centered, axis=1), "pix")
    unit = centered / jnp.sqrt(squares + EPS)[:, None]
    partial_gram = lax.dot_general(
        unit,
        lax.all_gather(unit, "frame", axis=0, tiled=True),
        (((1,), (1,)), ((), ())),
        precision=lax.Precision.HIGHEST,
        preferred_element_type=jnp.float32,
    )
    return lax.psum_scatter(partial_gram, "pix", scatter_dimension=1, tiled=True)


def solution(mesh):
    placed = (P("frame", "pix"), P("pix"))
    pair = mesh.shape["pix"] == 2 and mesh.shape["frame"] == 16
    return jax.shard_map(
        local_pair if pair else local,
        mesh=mesh, in_specs=placed, out_specs=P("frame", "pix"), check_vma=False,
    )
```

time: 271 us -> 215 us (0.79)
  waiting for transfers between devices: 212 us -> 98.3 us
  Pallas kernels: 0 us -> 73.6 us
  matrix products: 27.9 us -> 0 us
  starting transfers between devices: 0.04 us -> 25.5 us
  between operations: 13.4 us -> 1.49 us
  blocking collectives: 10.8 us -> 0 us
  local copies, waits for them, and re-layouts: 4.17 us -> 13.7 us
    reduce_scatter x1 -> x0, waiting for transfers between devices: 111 us -> none  [local(): lax.psum_scatter(partial_gram, 'pix', scatter_dimension=1, tiled=True)]
    all_gather x1 -> x0, waiting for transfers between devices: 101 us -> none  [local(): lax.all_gather(unit, 'frame', axis=0, tiled=True)]
    ppermute x0 -> x32, waiting for transfers between devices: none -> 98.3 us  [the longest x9 62.9 us: next_z(): lax.ppermute(a, 'frame', [(f, (f + 4) % frames) for f in range(frames)])]
    pallas_call x0 -> x15, Pallas kernels: none -> 73.6 us  [the longest x6 36.1 us: product(): pl.pallas_call(functools.partial(product_kernel, n), in_specs=[pl.BlockSp...]
    dot_general x1 -> x0, matrix products: 27.9 us -> none  [local(): lax.dot_general(unit, lax.all_gather(unit, 'frame', axis=0, tiled=True),...]
    ppermute x0 -> x32, starting transfers between devices: none -> 25.5 us  [the longest x8 12.7 us: swap_x(): return lax.ppermute(a, 'pix', [(0, 1), (1, 0)])]
    psum x2 -> x0, blocking collectives: 10.8 us -> none  [the longest x1 5.84 us: local(): total = lax.psum(jnp.sum(picked, axis=1), 'pix')]
    slice x0 -> x7, local copies, waits for them, and re-layouts: none -> 7.63 us  [the longest x3 4.58 us: local_pair(): from_core = swap_core(near[1:])]
  transfers between devices with their start and end apart: 2 -> 32, of which waited for: 2 -> 15; matrix products, arithmetic and copies ran while one was open for 0% -> 4% of each run, Pallas kernels for 0% -> 28%
where the time goes in v2:
time: 215 us; the launch traced here: 214 us
  waiting for transfers between devices  98.3 us (46%)
  Pallas kernels  73.6 us (34%)
  starting transfers between devices  25.5 us (12%)
  local copies, waits for them, and re-layouts  13.7 us (6%)
    ppermute x9, waiting for transfers between devices, next_z(): lax.ppermute(a, 'frame', [(f, (f + 4) % frames) for f in range(frames)])  62.9 us
    pallas_call x6, Pallas kernels, product(): pl.pallas_call(functools.partial(product_kernel, n), in_specs=[pl.BlockSp...  36.1 us
    ppermute x8, waiting for transfers between devices, swap_x(): return lax.ppermute(a, 'pix', [(0, 1), (1, 0)])  32.9 us
    pallas_call x3, Pallas kernels, place(): pl.pallas_call(place_kernel, grid_spec=pltpu.PrefetchScalarGridSpec(num_s...  16.4 us
    pallas_call x4, Pallas kernels, split_rows(): pl.pallas_call(rows_kernel, out_shape=[jax.ShapeDtypeStruct((rows, 2 * pi...  13.1 us
    ppermute x8, starting transfers between devices, swap_x(): return lax.ppermute(a, 'pix', [(0, 1), (1, 0)])  12.7 us
    ppermute x5, starting transfers between devices, swap_y(): return lax.ppermute(a, 'frame', [(f, f ^ 2) for f in range(frames)])  5.96 us
    pallas_call x1, Pallas kernels, pick(): pl.pallas_call(pick_kernel, out_shape=[jax.ShapeDtypeStruct((rows, pix),...  4.94 us
  transfers between devices with their start and end apart: 32, of which 15 were waited for; matrix products, arithmetic and copies ran while one was open for 4% of the time, Pallas kernels for 28%

profile of v2, /device:TPU:0, one launch (start us, length us, event | category | flops | bytes accessed | tf_op | source)
XLA Modules:
  0.0 214.4 jit_solution(831353605856349879)
XLA Ops:
  0.0 1.3 reshape.7.annulus_ref
  1.3 4.9 %pick.1 = (f32[384,768]{1,0:T(8,128)}, f32[8,768]{1,0:T(8,128)}) custom-call(s32[1,768]{1,0:T(1,128)} %reshape.7.annulus_ref, f32[384,1536]{1,0:T(8,128)} %library_ref.1), custom_call_target="tpu_custom_call" | custom-call | tf_op jit(solution)/shard_map/pick/pallas_call | solution.py:63
  6.2 2.9 %collective-permute-start = (f32[8,768]{1,0:T(8,128)}, f32[8,768]{1,0:T(8,128)S(1)}, u32[]{:S(2)}, u32[]{:S(2)}) collective-permute-start(f32[8,768]{1,0:T(8,128)} %get-tuple-element.20.mine_ref), channel_id=1, source_target_pairs={{0,1},{1,0},{2,3},{3,2},{4,5},{5,4},{6,7},{7,6},{8,9},{9,8},{10,11... | collective-permute-start | bytes 73736 | tf_op jit(solution)/shard_map/ppermute | solution.py:207
  9.1 2.0 collective-permute-done.other_ref
  11.2 0.6 copy-done.30
  11.8 3.1 %unit.1 = (f32[384,768]{1,0:T(8,128)}, f32[128,768]{1,0:T(8,128)}, f32[128,768]{1,0:T(8,128)}, f32[128,768]{1,0:T(8,128)}) custom-call(f32[384,768]{1,0:T(8,128)} %get-tuple-element.19.centered_ref, f32[8,768]{1,0:T(8,128)} %get-tuple-element.20.mine_ref, f32[8,768]{1,0:T(8,128)} %copy-done.30), custom_call_target="tpu_custom_call" | custom-call | tf_op jit(solution)/shard_map/unit/pallas_call | solution.py:91
  14.8 2.0 collective-permute-start.1
  16.9 1.5 collective-permute-start.9
  18.4 23.5 %collective-permute-done.1.b_ref = f32[384,768]{1,0:T(8,128)S(1)} collective-permute-done((f32[384,768]{1,0:T(8,128)}, f32[384,768]{1,0:T(8,128)S(1)}, u32[]{:S(2)}, u32[]{:S(2)}) %collective-permute-start.1) | collective-permute-done | bytes 1179680 | tf_op jit(solution)/shard_map/ppermute | solution.py:207
  41.9 1.8 collective-permute-start.10
  43.7 1.6 collective-permute-start.4
  45.2 1.6 collective-permute-start.16
  46.8 1.6 collective-permute-start.24
  48.4 9.3 %collective-permute-done.4.refs_7_ = f32[128,768]{1,0:T(8,128)S(1)} collective-permute-done((f32[128,768]{1,0:T(8,128)}, f32[128,768]{1,0:T(8,128)S(1)}, u32[]{:S(2)}, u32[]{:S(2)}) %collective-permute-start.4) | collective-permute-done | bytes 393248 | tf_op jit(solution)/shard_map/ppermute | solution.py:216
  57.7 8.4 %collective-permute-done.16.refs_7_ = f32[128,768]{1,0:T(8,128)S(1)} collective-permute-done((f32[128,768]{1,0:T(8,128)}, f32[128,768]{1,0:T(8,128)S(1)}, u32[]{:S(2)}, u32[]{:S(2)}) %collective-permute-start.16) | collective-permute-done | bytes 393248 | tf_op jit(solution)/shard_map/ppermute | solution.py:216
  66.1 8.4 %collective-permute-done.24.refs_7_ = f32[128,768]{1,0:T(8,128)S(1)} collective-permute-done((f32[128,768]{1,0:T(8,128)}, f32[128,768]{1,0:T(8,128)S(1)}, u32[]{:S(2)}, u32[]{:S(2)}) %collective-permute-start.24) | collective-permute-done | bytes 393248 | tf_op jit(solution)/shard_map/ppermute | solution.py:216
  74.6 0.6 fusion
  76.5 6.5 %collective-permute-done.5.refs_5_ = f32[128,768]{1,0:T(8,128)S(1)} collective-permute-done((f32[128,768]{1,0:T(8,128)S(1)}, f32[128,768]{1,0:T(8,128)S(1)}, u32[]{:S(2)}, u32[]{:S(2)}) %collective-permute-start.5) | collective-permute-done | bytes 393248 | tf_op jit(solution)/shard_map/ppermute | solution.py:216
  83.0 8.4 %collective-permute-done.17.refs_5_ = f32[128,768]{1,0:T(8,128)S(1)} collective-permute-done((f32[128,768]{1,0:T(8,128)S(1)}, f32[128,768]{1,0:T(8,128)S(1)}, u32[]{:S(2)}, u32[]{:S(2)}) %collective-permute-start.17) | collective-permute-done | bytes 393248 | tf_op jit(solution)/shard_map/ppermute | solution.py:216
  91.5 8.4 %collective-permute-done.25.refs_5_ = f32[128,768]{1,0:T(8,128)S(1)} collective-permute-done((f32[128,768]{1,0:T(8,128)S(1)}, f32[128,768]{1,0:T(8,128)S(1)}, u32[]{:S(2)}, u32[]{:S(2)}) %collective-permute-start.25) | collective-permute-done | bytes 393248 | tf_op jit(solution)/shard_map/ppermute | solution.py:216
  99.8 1.5 collective-permute-start.18
  101.4 0.5 collective-permute-start.12
  101.9 6.3 %collective-permute-done.7.refs_8_ = f32[128,768]{1,0:T(8,128)S(1)} collective-permute-done((f32[128,768]{1,0:T(8,128)S(1)}, f32[128,768]{1,0:T(8,128)S(1)}, u32[]{:S(2)}, u32[]{:S(2)}) %collective-permute-start.7) | collective-permute-done | bytes 393248 | tf_op jit(solution)/shard_map/ppermute | solution.py:216
  108.3 1.5 collective-permute-start.26
  109.8 3.5 %collective-permute-done.19.refs_8_ = f32[128,768]{1,0:T(8,128)S(1)} collective-permute-done((f32[128,768]{1,0:T(8,128)S(1)}, f32[128,768]{1,0:T(8,128)S(1)}, u32[]{:S(2)}, u32[]{:S(2)}) %collective-permute-start.19) | collective-permute-done | bytes 393248 | tf_op jit(solution)/shard_map/ppermute | solution.py:216
  113.4 1.6 collective-permute-start.20
  115.1 4.3 %collective-permute-done.26.refs_6_ = f32[128,768]{1,0:T(8,128)S(1)} collective-permute-done((f32[128,768]{1,0:T(8,128)S(1)}, f32[128,768]{1,0:T(8,128)S(1)}, u32[]{:S(2)}, u32[]{:S(2)}) %collective-permute-start.26) | collective-permute-done | bytes 393248 | tf_op jit(solution)/shard_map/ppermute | solution.py:207
  119.3 3.6 %collective-permute-done.27.refs_8_ = f32[128,768]{1,0:T(8,128)S(1)} collective-permute-done((f32[128,768]{1,0:T(8,128)S(1)}, f32[128,768]{1,0:T(8,128)S(1)}, u32[]{:S(2)}, u32[]{:S(2)}) %collective-permute-start.27) | collective-permute-done | bytes 393248 | tf_op jit(solution)/shard_map/ppermute | solution.py:216
  122.9 0.9 broadcast_select_fusion
  123.8 0.7 collective-permute-done.20.refs_9_
  124.5 1.5 collective-permute-start.28
  126.1 0.6 collective-permute-start.6
  127.1 1.0 copy-done.23
  128.1 1.1 collective-permute-start.8
  129.2 3.3 %split_rows.6 = (bf16[384,1536]{1,0:T(8,128)(2,1)}, bf16[384,1536]{1,0:T(8,128)(2,1)}) custom-call(f32[384,768]{1,0:T(8,128)} %collective-permute-done.9.a_ref, f32[384,768]{1,0:T(8,128)} %collective-permute-done.10.b_ref), custom_call_target="tpu_custom_call" | custom-call | flops 1769472 | bytes 4718592 | tf_op jit(solution)/shard_map/split_rows/pallas_call | solution.py:108
  132.5 3.2 %split_rows.7 = (bf16[384,1536]{1,0:T(8,128)(2,1)}, bf16[384,1536]{1,0:T(8,128)(2,1)}) custom-call(f32[384,768]{1,0:T(8,128)} %copy-done.22, f32[384,768]{1,0:T(8,128)} %copy-done.23), custom_call_target="tpu_custom_call" | custom-call | flops 1769472 | bytes 4718592 | tf_op jit(solution)/shard_map/split_rows/pallas_call | solution.py:108
  135.8 6.0 %product.9 = f32[2,384,256]{2,1,0:T(8,128)} custom-call(s32[2]{0:T(128)} %copy-done.29, bf16[384,1536]{1,0:T(8,128)(2,1)} %get-tuple-element.27.refs_0_, bf16[384,1536]{1,0:T(8,128)(2,1)} %get-tuple-element.28.refs_1_, bf16[384,1536]{1,0:T(8,128)(2,1)} %get-tuple-element.29.refs_2_, bf16[384,1536]{1,0:T(8,128)(2,1)} %get-tuple-element.30.refs_3_, ...), custom_call_target="tpu_custom_call" | custom-call | flops 1811939328 | bytes 5505024 | tf_op jit(solution)/shard_map/product/pallas_call | solution.py:145
  141.8 0.6 collective-permute-start.21
  142.5 6.0 %product.11 = f32[2,384,256]{2,1,0:T(8,128)} custom-call(s32[2]{0:T(128)} %copy-done.29, bf16[384,1536]{1,0:T(8,128)(2,1)} %get-tuple-element.27.refs_0_, bf16[384,1536]{1,0:T(8,128)(2,1)} %get-tuple-element.28.refs_1_, bf16[384,1536]{1,0:T(8,128)(2,1)} %get-tuple-element.29.refs_2_, bf16[384,1536]{1,0:T(8,128)(2,1)} %get-tuple-element.30.refs_3_, ...), custom_call_target="tpu_custom_call" | custom-call | flops 1811939328 | bytes 5505024 | tf_op jit(solution)/shard_map/product/pallas_call | solution.py:145
  148.5 1.4 collective-permute-start.29
  149.9 2.4 %collective-permute-done.8.refs_9_ = f32[128,768]{1,0:T(8,128)S(1)} collective-permute-done((f32[128,768]{1,0:T(8,128)S(1)}, f32[128,768]{1,0:T(8,128)S(1)}, u32[]{:S(2)}, u32[]{:S(2)}) %collective-permute-start.8) | collective-permute-done | bytes 393248 | tf_op jit(solution)/shard_map/ppermute | solution.py:207
  152.4 0.8 copy-done.19
  153.1 6.0 %product.7 = f32[2,384,256]{2,1,0:T(8,128)} custom-call(s32[2]{0:T(128)} %copy-done.29, bf16[384,1536]{1,0:T(8,128)(2,1)} %get-tuple-element.27.refs_0_, bf16[384,1536]{1,0:T(8,128)(2,1)} %get-tuple-element.28.refs_1_, bf16[384,1536]{1,0:T(8,128)(2,1)} %get-tuple-element.29.refs_2_, bf16[384,1536]{1,0:T(8,128)(2,1)} %get-tuple-element.30.refs_3_, ...), custom_call_target="tpu_custom_call" | custom-call | flops 1811939328 | bytes 5505024 | tf_op jit(solution)/shard_map/product/pallas_call | solution.py:145
  159.2 0.7 collective-permute-start.13
  159.8 3.2 %split_rows.4 = (bf16[384,1536]{1,0:T(8,128)(2,1)}, bf16[384,1536]{1,0:T(8,128)(2,1)}) custom-call(f32[384,768]{1,0:T(8,128)} %get-tuple-element.21.a_ref, f32[384,768]{1,0:T(8,128)} %copy-done.21), custom_call_target="tpu_custom_call" | custom-call | flops 1769472 | bytes 4718592 | tf_op jit(solution)/shard_map/split_rows/pallas_call | solution.py:108
  163.1 3.3 %split_rows.5 = (bf16[384,1536]{1,0:T(8,128)(2,1)}, bf16[384,1536]{1,0:T(8,128)(2,1)}) custom-call(f32[384,768]{1,0:T(8,128)} %collective-permute-done.2.a_ref, f32[384,768]{1,0:T(8,128)} %collective-permute-done.3.b_ref), custom_call_target="tpu_custom_call" | custom-call | flops 1769472 | bytes 4718592 | tf_op jit(solution)/shard_map/split_rows/pallas_call | solution.py:108
  166.4 6.0 %product.10.own_ref = f32[2,384,256]{2,1,0:T(8,128)} custom-call(s32[2]{0:T(128)} %copy-done.29, bf16[384,1536]{1,0:T(8,128)(2,1)} %get-tuple-element.22.refs_0_, bf16[384,1536]{1,0:T(8,128)(2,1)} %get-tuple-element.23.refs_1_, bf16[384,1536]{1,0:T(8,128)(2,1)} %get-tuple-element.24.refs_2_, bf16[384,1536]{1,0:T(8,128)(2,1)} %get-tuple-element.25.refs_3_, ...), custom_call_target="tpu_custom_call" | custom-call | flops 1811939328 | bytes 5505024 | tf_op jit(solution)/shard_map/product/pallas_call | solution.py:145
  172.4 1.0 slice.40
  173.5 6.0 %product.6.own_ref = f32[2,384,256]{2,1,0:T(8,128)} custom-call(s32[2]{0:T(128)} %copy-done.29, bf16[384,1536]{1,0:T(8,128)(2,1)} %get-tuple-element.22.refs_0_, bf16[384,1536]{1,0:T(8,128)(2,1)} %get-tuple-element.23.refs_1_, bf16[384,1536]{1,0:T(8,128)(2,1)} %get-tuple-element.24.refs_2_, bf16[384,1536]{1,0:T(8,128)(2,1)} %get-tuple-element.25.refs_3_, ...), custom_call_target="tpu_custom_call" | custom-call | flops 1811939328 | bytes 5505024 | tf_op jit(solution)/shard_map/product/pallas_call | solution.py:145
  179.5 1.8 slice.36
  181.3 6.0 %product.8.own_ref = f32[2,384,256]{2,1,0:T(8,128)} custom-call(s32[2]{0:T(128)} %copy-done.29, bf16[384,1536]{1,0:T(8,128)(2,1)} %get-tuple-element.22.refs_0_, bf16[384,1536]{1,0:T(8,128)(2,1)} %get-tuple-element.23.refs_1_, bf16[384,1536]{1,0:T(8,128)(2,1)} %get-tuple-element.24.refs_2_, bf16[384,1536]{1,0:T(8,128)(2,1)} %get-tuple-element.25.refs_3_, ...), custom_call_target="tpu_custom_call" | custom-call | flops 1811939328 | bytes 5505024 | tf_op jit(solution)/shard_map/product/pallas_call | solution.py:145
  187.3 1.8 slice.38
  189.1 0.5 collective-permute-start.22
  189.6 0.8 slice.41
  190.4 0.8 slice.39
  191.7 2.4 %collective-permute-done.13.y_ref = f32[2,384,256]{2,1,0:T(8,128)S(1)} collective-permute-done((f32[2,384,256]{2,1,0:T(8,128)}, f32[2,384,256]{2,1,0:T(8,128)S(1)}, u32[]{:S(2)}, u32[]{:S(2)}) %collective-permute-start.13) | collective-permute-done | bytes 786464 | tf_op jit(solution)/shard_map/ppermute | solution.py:210
  194.2 0.8 slice.37
  195.0 0.5 collective-permute-start.15
  195.6 0.6 broadcast_add_fusion
  196.2 5.5 %place.3.refs_0_ = f32[384,3072]{1,0:T(8,128)} custom-call(s32[8]{0:T(128)} %copy-done.31, f32[2,384,256]{2,1,0:T(8,128)} %product.10.own_ref, f32[2,384,256]{2,1,0:T(8,128)} %copy-done.13, f32[1,384,256]{2,1,0:T(8,128)} %copy-done.24, f32[1,384,256]{2,1,0:T(8,128)} %collective-permute-done.31.both_ref), custom_call_target="tpu_custom_call" | custom-call | bytes 3145728 | tf_op jit(solution)/shard_map/place/pallas_call | solution.py:181
  201.7 0.7 copy-done.25
  202.6 5.5 %place.4.refs_0_ = f32[384,3072]{1,0:T(8,128)} custom-call(s32[8]{0:T(128)} %get-tuple-element.33.at_ref, f32[2,384,256]{2,1,0:T(8,128)} %product.8.own_ref, f32[2,384,256]{2,1,0:T(8,128)} %copy-done.11, f32[1,384,256]{2,1,0:T(8,128)} %copy-done.25, f32[1,384,256]{2,1,0:T(8,128)} %copy-done.27, f32[384,3072]{1,0:T(8,128)} %place.3.refs_0_), custom_call_target="tpu_custom_call", output_to_operand_aliasing={{}: (5, {})} | custom-call | bytes 3145728 | tf_op jit(solution)/shard_map/place/pallas_call | solution.py:181
  208.1 0.7 copy-done.26
  208.9 5.5 %place.5 = f32[384,3072]{1,0:T(8,128)} custom-call(s32[8]{0:T(128)} %get-tuple-element.34.at_ref, f32[2,384,256]{2,1,0:T(8,128)} %product.6.own_ref, f32[2,384,256]{2,1,0:T(8,128)} %copy-done.12, f32[1,384,256]{2,1,0:T(8,128)} %copy-done.26, f32[1,384,256]{2,1,0:T(8,128)} %copy-done.28, f32[384,3072]{1,0:T(8,128)} %place.4.refs_0_), custom_call_target="tpu_custom_call", output_to_operand_aliasing={{}: (5, {})} | custom-call | bytes 3145728 | tf_op jit(solution)/shard_map/place/pallas_call | solution.py:181
  (96 shorter events, 2.0 us)
Async XLA Ops:
  6.2 5.0 %collective-permute-start = (f32[8,768]{1,0:T(8,128)}, f32[8,768]{1,0:T(8,128)S(1)}, u32[]{:S(2)}, u32[]{:S(2)}) collective-permute-start(f32[8,768]{1,0:T(8,128)} %get-tuple-element.20.mine_ref), channel_id=1, source_target_pairs={{0,1},{1,0},{2,3},{3,2},{4,5},{5,4},{6,7},{7,6},{8,9},{9,8},{10,11... | collective-permute-start | bytes 73736 | tf_op jit(solution)/shard_map/ppermute | solution.py:207
  11.2 0.6 copy-start.30
  14.8 87.0 %copy-start.1 = (f32[128,768]{1,0:T(8,128)S(1)}, f32[128,768]{1,0:T(8,128)}, u32[]{:S(2)}) copy-start(f32[128,768]{1,0:T(8,128)} %get-tuple-element.32.refs_4_) | copy-start | bytes 1179652
  14.8 27.1 %collective-permute-start.1 = (f32[384,768]{1,0:T(8,128)}, f32[384,768]{1,0:T(8,128)S(1)}, u32[]{:S(2)}, u32[]{:S(2)}) collective-permute-start(f32[384,768]{1,0:T(8,128)} %get-tuple-element.21.a_ref), channel_id=1, source_target_pairs={{0,1},{1,0},{2,3},{3,2},{4,5},{5,4},{6,7},{7,6},{8,9},{9,8},{10,11... | collective-permute-start | bytes 3538952 | tf_op jit(solution)/shard_map/ppermute | solution.py:207
  16.9 84.5 %collective-permute-start.9 = (f32[384,768]{1,0:T(8,128)}, f32[384,768]{1,0:T(8,128)}, u32[]{:S(2)}, u32[]{:S(2)}) collective-permute-start(f32[384,768]{1,0:T(8,128)} %get-tuple-element.21.a_ref), channel_id=1, source_target_pairs={{0,4},{2,6},{4,0},{6,2},{8,12},{10,14},{12,8},{14,10},{16,20},{18,... | collective-permute-start | bytes 3538952 | tf_op jit(solution)/shard_map/ppermute | solution.py:210
  41.9 84.1 %copy-start.21 = (f32[384,768]{1,0:T(8,128)}, f32[384,768]{1,0:T(8,128)S(1)}, u32[]{:S(2)}) copy-start(f32[384,768]{1,0:T(8,128)S(1)} %collective-permute-done.1.b_ref) | copy-start | bytes 3538948
  41.9 59.5 %collective-permute-start.10 = (f32[384,768]{1,0:T(8,128)S(1)}, f32[384,768]{1,0:T(8,128)}, u32[]{:S(2)}, u32[]{:S(2)}) collective-permute-start(f32[384,768]{1,0:T(8,128)S(1)} %collective-permute-done.1.b_ref), channel_id=1, source_target_pairs={{0,4},{2,6},{4,0},{6,2},{8,12},{10,14},{12,8},{14,10},{16,20},{18,... | collective-permute-start | bytes 3538952 | tf_op jit(solution)/shard_map/ppermute | solution.py:210
  43.7 14.1 %collective-permute-start.4 = (f32[128,768]{1,0:T(8,128)}, f32[128,768]{1,0:T(8,128)S(1)}, u32[]{:S(2)}, u32[]{:S(2)}) collective-permute-start(f32[128,768]{1,0:T(8,128)} %get-tuple-element.26.refs_4_), channel_id=1, source_target_pairs={{0,8},{2,10},{4,12},{6,14},{8,16},{10,18},{12,20},{14,22},{16,24},... | collective-permute-start | bytes 1179656 | tf_op jit(solution)/shard_map/ppermute | solution.py:216
  45.2 20.9 %collective-permute-start.16 = (f32[128,768]{1,0:T(8,128)}, f32[128,768]{1,0:T(8,128)S(1)}, u32[]{:S(2)}, u32[]{:S(2)}) collective-permute-start(f32[128,768]{1,0:T(8,128)} %get-tuple-element.31.refs_4_), channel_id=1, source_target_pairs={{0,8},{2,10},{4,12},{6,14},{8,16},{10,18},{12,20},{14,22},{16,24},... | collective-permute-start | bytes 1179656 | tf_op jit(solution)/shard_map/ppermute | solution.py:216
  46.8 27.8 %collective-permute-start.24 = (f32[128,768]{1,0:T(8,128)}, f32[128,768]{1,0:T(8,128)S(1)}, u32[]{:S(2)}, u32[]{:S(2)}) collective-permute-start(f32[128,768]{1,0:T(8,128)} %get-tuple-element.32.refs_4_), channel_id=1, source_target_pairs={{0,8},{2,10},{4,12},{6,14},{8,16},{10,18},{12,20},{14,22},{16,24},... | collective-permute-start | bytes 1179656 | tf_op jit(solution)/shard_map/ppermute | solution.py:216
  57.7 68.3 %copy-start.3 = (f32[128,768]{1,0:T(8,128)}, f32[128,768]{1,0:T(8,128)S(1)}, u32[]{:S(2)}) copy-start(f32[128,768]{1,0:T(8,128)S(1)} %collective-permute-done.4.refs_7_) | copy-start | bytes 1179652
  57.7 25.3 %collective-permute-start.5 = (f32[128,768]{1,0:T(8,128)S(1)}, f32[128,768]{1,0:T(8,128)S(1)}, u32[]{:S(2)}, u32[]{:S(2)}) collective-permute-start(f32[128,768]{1,0:T(8,128)S(1)} %collective-permute-done.4.refs_7_), channel_id=1, source_target_pairs={{0,8},{2,10},{4,12},{6,14},{8,16},{10,18},{12,20},{14,22},{16,24},... | collective-permute-start | bytes 1179656 | tf_op jit(solution)/shard_map/ppermute | solution.py:216
  66.1 47.2 %copy-start.2 = (f32[128,768]{1,0:T(8,128)}, f32[128,768]{1,0:T(8,128)S(1)}, u32[]{:S(2)}) copy-start(f32[128,768]{1,0:T(8,128)S(1)} %collective-permute-done.16.refs_7_) | copy-start | bytes 1179652
  66.1 25.3 %collective-permute-start.17 = (f32[128,768]{1,0:T(8,128)S(1)}, f32[128,768]{1,0:T(8,128)S(1)}, u32[]{:S(2)}, u32[]{:S(2)}) collective-permute-start(f32[128,768]{1,0:T(8,128)S(1)} %collective-permute-done.16.refs_7_), channel_id=1, source_target_pairs={{0,8},{2,10},{4,12},{6,14},{8,16},{10,18},{12,20},{14,22},{16,24},... | collective-permute-start | bytes 1179656 | tf_op jit(solution)/shard_map/ppermute | solution.py:216
  74.6 48.3 %copy-start.6 = (f32[128,768]{1,0:T(8,128)}, f32[128,768]{1,0:T(8,128)S(1)}, u32[]{:S(2)}) copy-start(f32[128,768]{1,0:T(8,128)S(1)} %collective-permute-done.24.refs_7_) | copy-start | bytes 1179652
  74.6 25.3 %collective-permute-start.25 = (f32[128,768]{1,0:T(8,128)S(1)}, f32[128,768]{1,0:T(8,128)S(1)}, u32[]{:S(2)}, u32[]{:S(2)}) collective-permute-start(f32[128,768]{1,0:T(8,128)S(1)} %collective-permute-done.24.refs_7_), channel_id=1, source_target_pairs={{0,8},{2,10},{4,12},{6,14},{8,16},{10,18},{12,20},{14,22},{16,24},... | collective-permute-start | bytes 1179656 | tf_op jit(solution)/shard_map/ppermute | solution.py:216
  74.6 27.3 %copy-start.29 = (s32[2]{0:T(128)}, s32[2]{0:T(128)S(1)}, u32[]{:S(2)}) copy-start(s32[2]{0:T(128)S(1)} %add_convert_fusion.choice_ref) | copy-start | bytes 28
  83.0 32.0 %copy-start.5 = (f32[128,768]{1,0:T(8,128)}, f32[128,768]{1,0:T(8,128)S(1)}, u32[]{:S(2)}) copy-start(f32[128,768]{1,0:T(8,128)S(1)} %collective-permute-done.5.refs_5_) | copy-start | bytes 1179652
  83.0 25.3 %collective-permute-start.7 = (f32[128,768]{1,0:T(8,128)S(1)}, f32[128,768]{1,0:T(8,128)S(1)}, u32[]{:S(2)}, u32[]{:S(2)}) collective-permute-start(f32[128,768]{1,0:T(8,128)S(1)} %collective-permute-done.5.refs_5_), channel_id=1, source_target_pairs={{0,8},{2,10},{4,12},{6,14},{8,16},{10,18},{12,20},{14,22},{16,24},... | collective-permute-start | bytes 1179656 | tf_op jit(solution)/shard_map/ppermute | solution.py:216
  91.4 10.5 %copy-start.4 = (f32[128,768]{1,0:T(8,128)}, f32[128,768]{1,0:T(8,128)S(1)}, u32[]{:S(2)}) copy-start(f32[128,768]{1,0:T(8,128)S(1)} %collective-permute-done.17.refs_5_) | copy-start | bytes 1179652
  91.4 21.9 %collective-permute-start.19 = (f32[128,768]{1,0:T(8,128)S(1)}, f32[128,768]{1,0:T(8,128)S(1)}, u32[]{:S(2)}, u32[]{:S(2)}) collective-permute-start(f32[128,768]{1,0:T(8,128)S(1)} %collective-permute-done.17.refs_5_), channel_id=1, source_target_pairs={{0,8},{2,10},{4,12},{6,14},{8,16},{10,18},{12,20},{14,22},{16,24},... | collective-permute-start | bytes 1179656 | tf_op jit(solution)/shard_map/ppermute | solution.py:216
  91.5 23.5 %copy-start = (f32[128,768]{1,0:T(8,128)S(1)}, f32[128,768]{1,0:T(8,128)}, u32[]{:S(2)}) copy-start(f32[128,768]{1,0:T(8,128)} %get-tuple-element.26.refs_4_) | copy-start | bytes 1179652
  99.8 13.5 %copy-start.7 = (f32[128,768]{1,0:T(8,128)}, f32[128,768]{1,0:T(8,128)S(1)}, u32[]{:S(2)}) copy-start(f32[128,768]{1,0:T(8,128)S(1)} %collective-permute-done.25.refs_5_) | copy-start | bytes 1179652
  99.8 13.5 %collective-permute-start.18 = (f32[128,768]{1,0:T(8,128)S(1)}, f32[128,768]{1,0:T(8,128)S(1)}, u32[]{:S(2)}, u32[]{:S(2)}) collective-permute-start(f32[128,768]{1,0:T(8,128)S(1)} %broadcast_select_fusion.4), channel_id=1, source_target_pairs={{0,1},{1,0},{2,3},{3,2},{4,5},{5,4},{6,7},{7,6},{8,9},{9,8},{10,11... | collective-permute-start | bytes 1179656 | tf_op jit(solution)/shard_map/ppermute | solution.py:207
  101.3 24.7 %collective-permute-start.11 = (f32[384,768]{1,0:T(8,128)}, f32[384,768]{1,0:T(8,128)S(1)}, u32[]{:S(2)}, u32[]{:S(2)}) collective-permute-start(f32[384,768]{1,0:T(8,128)} %collective-permute-done.9.a_ref), channel_id=1, source_target_pairs={{0,2},{2,0},{4,6},{6,4},{8,10},{10,8},{12,14},{14,12},{16,18},{18,... | collective-permute-start | bytes 3538952 | tf_op jit(solution)/shard_map/ppermute | solution.py:213
  101.4 25.7 %collective-permute-start.12 = (f32[384,768]{1,0:T(8,128)}, f32[384,768]{1,0:T(8,128)S(1)}, u32[]{:S(2)}, u32[]{:S(2)}) collective-permute-start(f32[384,768]{1,0:T(8,128)} %collective-permute-done.10.b_ref), channel_id=1, source_target_pairs={{0,2},{2,0},{4,6},{6,4},{8,10},{10,8},{12,14},{14,12},{16,18},{18,... | collective-permute-start | bytes 3538952 | tf_op jit(solution)/shard_map/ppermute | solution.py:213
  108.3 17.7 %copy-start.9 = (f32[128,768]{1,0:T(8,128)}, f32[128,768]{1,0:T(8,128)S(1)}, u32[]{:S(2)}) copy-start(f32[128,768]{1,0:T(8,128)S(1)} %collective-permute-done.7.refs_8_) | copy-start | bytes 1179652
  108.3 11.0 %collective-permute-start.26 = (f32[128,768]{1,0:T(8,128)S(1)}, f32[128,768]{1,0:T(8,128)S(1)}, u32[]{:S(2)}, u32[]{:S(2)}) collective-permute-start(f32[128,768]{1,0:T(8,128)S(1)} %broadcast_select_fusion.3), channel_id=1, source_target_pairs={{0,1},{1,0},{2,3},{3,2},{4,5},{5,4},{6,7},{7,6},{8,9},{9,8},{10,11... | collective-permute-start | bytes 1179656 | tf_op jit(solution)/shard_map/ppermute | solution.py:207
  113.3 1.7 copy-start.8
  113.3 9.6 %collective-permute-start.27 = (f32[128,768]{1,0:T(8,128)S(1)}, f32[128,768]{1,0:T(8,128)S(1)}, u32[]{:S(2)}, u32[]{:S(2)}) collective-permute-start(f32[128,768]{1,0:T(8,128)S(1)} %collective-permute-done.25.refs_5_), channel_id=1, source_target_pairs={{0,8},{2,10},{4,12},{6,14},{8,16},{10,18},{12,20},{14,22},{16,24},... | collective-permute-start | bytes 1179656 | tf_op jit(solution)/shard_map/ppermute | solution.py:216
  113.3 6.0 %copy-start.20 = (f32[384,768]{1,0:T(8,128)S(1)}, f32[384,768]{1,0:T(8,128)}, u32[]{:S(2)}) copy-start(f32[384,768]{1,0:T(8,128)} %get-tuple-element.21.a_ref) | copy-start | bytes 3538948
  113.4 10.4 %copy-start.14 = (f32[128,768]{1,0:T(8,128)}, f32[128,768]{1,0:T(8,128)S(1)}, u32[]{:S(2)}) copy-start(f32[128,768]{1,0:T(8,128)S(1)} %collective-permute-done.18.refs_6_) | copy-start | bytes 1179652
  113.4 11.1 %collective-permute-start.20 = (f32[128,768]{1,0:T(8,128)S(1)}, f32[128,768]{1,0:T(8,128)S(1)}, u32[]{:S(2)}, u32[]{:S(2)}) collective-permute-start(f32[128,768]{1,0:T(8,128)S(1)} %broadcast_select_fusion.1), channel_id=1, source_target_pairs={{0,1},{1,0},{2,3},{3,2},{4,5},{5,4},{6,7},{7,6},{8,9},{9,8},{10,11... | collective-permute-start | bytes 1179656 | tf_op jit(solution)/shard_map/ppermute | solution.py:207
  119.3 6.7 %copy-start.16 = (f32[128,768]{1,0:T(8,128)}, f32[128,768]{1,0:T(8,128)S(1)}, u32[]{:S(2)}) copy-start(f32[128,768]{1,0:T(8,128)S(1)} %collective-permute-done.26.refs_6_) | copy-start | bytes 1179652
  119.3 43.8 %collective-permute-start.2 = (f32[384,768]{1,0:T(8,128)S(1)}, f32[384,768]{1,0:T(8,128)}, u32[]{:S(2)}, u32[]{:S(2)}) collective-permute-start(f32[384,768]{1,0:T(8,128)S(1)} %copy-done.20), channel_id=1, source_target_pairs={{0,2},{2,0},{4,6},{6,4},{8,10},{10,8},{12,14},{14,12},{16,18},{18,... | collective-permute-start | bytes 3538952 | tf_op jit(solution)/shard_map/ppermute | solution.py:213
  122.9 3.2 %copy-start.10 = (f32[128,768]{1,0:T(8,128)}, f32[128,768]{1,0:T(8,128)S(1)}, u32[]{:S(2)}) copy-start(f32[128,768]{1,0:T(8,128)S(1)} %collective-permute-done.27.refs_8_) | copy-start | bytes 1179652
  122.9 40.2 %collective-permute-start.3 = (f32[384,768]{1,0:T(8,128)S(1)}, f32[384,768]{1,0:T(8,128)}, u32[]{:S(2)}, u32[]{:S(2)}) collective-permute-start(f32[384,768]{1,0:T(8,128)S(1)} %collective-permute-done.1.b_ref), channel_id=1, source_target_pairs={{0,2},{2,0},{4,6},{6,4},{8,10},{10,8},{12,14},{14,12},{16,18},{18,... | collective-permute-start | bytes 3538952 | tf_op jit(solution)/shard_map/ppermute | solution.py:213
  124.5 8.0 %copy-start.15 = (f32[128,768]{1,0:T(8,128)}, f32[128,768]{1,0:T(8,128)S(1)}, u32[]{:S(2)}) copy-start(f32[128,768]{1,0:T(8,128)S(1)} %collective-permute-done.20.refs_9_) | copy-start | bytes 1179652
  124.5 17.3 %collective-permute-start.28 = (f32[128,768]{1,0:T(8,128)}, f32[128,768]{1,0:T(8,128)S(1)}, u32[]{:S(2)}, u32[]{:S(2)}) collective-permute-start(f32[128,768]{1,0:T(8,128)} %broadcast_select_fusion), channel_id=1, source_target_pairs={{0,1},{1,0},{2,3},{3,2},{4,5},{5,4},{6,7},{7,6},{8,9},{9,8},{10,11... | collective-permute-start | bytes 1179656 | tf_op jit(solution)/shard_map/ppermute | solution.py:207
  126.1 1.0 copy-start.22
  126.1 22.5 %collective-permute-start.6 = (f32[128,768]{1,0:T(8,128)S(1)}, f32[128,768]{1,0:T(8,128)S(1)}, u32[]{:S(2)}, u32[]{:S(2)}) collective-permute-start(f32[128,768]{1,0:T(8,128)S(1)} %broadcast_select_fusion.5), channel_id=1, source_target_pairs={{0,1},{1,0},{2,3},{3,2},{4,5},{5,4},{6,7},{7,6},{8,9},{9,8},{10,11... | collective-permute-start | bytes 1179656 | tf_op jit(solution)/shard_map/ppermute | solution.py:207
  127.1 1.0 copy-start.23
  128.1 24.3 %collective-permute-start.8 = (f32[128,768]{1,0:T(8,128)S(1)}, f32[128,768]{1,0:T(8,128)S(1)}, u32[]{:S(2)}, u32[]{:S(2)}) collective-permute-start(f32[128,768]{1,0:T(8,128)S(1)} %broadcast_select_fusion.2), channel_id=1, source_target_pairs={{0,1},{1,0},{2,3},{3,2},{4,5},{5,4},{6,7},{7,6},{8,9},{9,8},{10,11... | collective-permute-start | bytes 1179656 | tf_op jit(solution)/shard_map/ppermute | solution.py:207
  141.8 0.8 copy-start.18
  141.8 48.7 %collective-permute-start.21 = (f32[2,384,256]{2,1,0:T(8,128)}, f32[2,384,256]{2,1,0:T(8,128)S(1)}, u32[]{:S(2)}, u32[]{:S(2)}) collective-permute-start(f32[2,384,256]{2,1,0:T(8,128)} %product.9), channel_id=1, source_target_pairs={{0,4},{2,6},{4,0},{6,2},{8,12},{10,14},{12,8},{14,10},{16,20},{18,... | collective-permute-start | bytes 2359304 | tf_op jit(solution)/shard_map/ppermute | solution.py:210
  148.5 3.8 %copy-start.17 = (f32[128,768]{1,0:T(8,128)}, f32[128,768]{1,0:T(8,128)S(1)}, u32[]{:S(2)}) copy-start(f32[128,768]{1,0:T(8,128)S(1)} %collective-permute-done.6.refs_6_) | copy-start | bytes 1179652
  148.5 41.0 %collective-permute-start.29 = (f32[2,384,256]{2,1,0:T(8,128)}, f32[2,384,256]{2,1,0:T(8,128)S(1)}, u32[]{:S(2)}, u32[]{:S(2)}) collective-permute-start(f32[2,384,256]{2,1,0:T(8,128)} %product.11), channel_id=1, source_target_pairs={{0,4},{2,6},{4,0},{6,2},{8,12},{10,14},{12,8},{14,10},{16,20},{18,... | collective-permute-start | bytes 2359304 | tf_op jit(solution)/shard_map/ppermute | solution.py:210
  152.4 0.8 copy-start.19
  159.2 35.0 %collective-permute-start.13 = (f32[2,384,256]{2,1,0:T(8,128)}, f32[2,384,256]{2,1,0:T(8,128)S(1)}, u32[]{:S(2)}, u32[]{:S(2)}) collective-permute-start(f32[2,384,256]{2,1,0:T(8,128)} %product.7), channel_id=1, source_target_pairs={{0,4},{2,6},{4,0},{6,2},{8,12},{10,14},{12,8},{14,10},{16,20},{18,... | collective-permute-start | bytes 2359304 | tf_op jit(solution)/shard_map/ppermute | solution.py:210
  173.5 21.5 %collective-permute-start.30 = (f32[1,384,256]{2,1,0:T(8,128)S(1)}, f32[1,384,256]{2,1,0:T(8,128)S(1)}, u32[]{:S(2)}, u32[]{:S(2)}) collective-permute-start(f32[1,384,256]{2,1,0:T(8,128)S(1)} %slice.40), channel_id=1, source_target_pairs={{0,2},{2,0},{4,6},{6,4},{8,10},{10,8},{12,14},{14,12},{16,18},{18,... | collective-permute-start | bytes 1179656 | tf_op jit(solution)/shard_map/ppermute | solution.py:213
  189.1 12.6 %collective-permute-start.22 = (f32[1,384,256]{2,1,0:T(8,128)}, f32[1,384,256]{2,1,0:T(8,128)S(1)}, u32[]{:S(2)}, u32[]{:S(2)}) collective-permute-start(f32[1,384,256]{2,1,0:T(8,128)} %slice.38), channel_id=1, source_target_pairs={{0,2},{2,0},{4,6},{6,4},{8,10},{10,8},{12,14},{14,12},{16,18},{18,... | collective-permute-start | bytes 1179656 | tf_op jit(solution)/shard_map/ppermute | solution.py:213
  189.6 5.4 %copy-start.13 = (f32[2,384,256]{2,1,0:T(8,128)}, f32[2,384,256]{2,1,0:T(8,128)S(1)}, u32[]{:S(2)}) copy-start(f32[2,384,256]{2,1,0:T(8,128)S(1)} %collective-permute-done.29.y_ref) | copy-start | bytes 2359300
  190.4 5.8 %collective-permute-start.31 = (f32[1,384,256]{2,1,0:T(8,128)}, f32[1,384,256]{2,1,0:T(8,128)}, u32[]{:S(2)}, u32[]{:S(2)}) collective-permute-start(f32[1,384,256]{2,1,0:T(8,128)} %slice.41), channel_id=1, source_target_pairs={{0,2},{2,0},{4,6},{6,4},{8,10},{10,8},{12,14},{14,12},{16,18},{18,... | collective-permute-start | bytes 1179656 | tf_op jit(solution)/shard_map/ppermute | solution.py:213
  190.4 11.3 %copy-start.11 = (f32[2,384,256]{2,1,0:T(8,128)}, f32[2,384,256]{2,1,0:T(8,128)S(1)}, u32[]{:S(2)}) copy-start(f32[2,384,256]{2,1,0:T(8,128)S(1)} %collective-permute-done.21.y_ref) | copy-start | bytes 2359300
  191.2 10.5 %collective-permute-start.23 = (f32[1,384,256]{2,1,0:T(8,128)}, f32[1,384,256]{2,1,0:T(8,128)S(1)}, u32[]{:S(2)}, u32[]{:S(2)}) collective-permute-start(f32[1,384,256]{2,1,0:T(8,128)} %slice.39), channel_id=1, source_target_pairs={{0,2},{2,0},{4,6},{6,4},{8,10},{10,8},{12,14},{14,12},{16,18},{18,... | collective-permute-start | bytes 1179656 | tf_op jit(solution)/shard_map/ppermute | solution.py:213
  194.2 7.5 %copy-start.12 = (f32[2,384,256]{2,1,0:T(8,128)}, f32[2,384,256]{2,1,0:T(8,128)S(1)}, u32[]{:S(2)}) copy-start(f32[2,384,256]{2,1,0:T(8,128)S(1)} %collective-permute-done.13.y_ref) | copy-start | bytes 2359300
  194.2 13.9 %collective-permute-start.14 = (f32[1,384,256]{2,1,0:T(8,128)}, f32[1,384,256]{2,1,0:T(8,128)S(1)}, u32[]{:S(2)}, u32[]{:S(2)}) collective-permute-start(f32[1,384,256]{2,1,0:T(8,128)} %slice.36), channel_id=1, source_target_pairs={{0,2},{2,0},{4,6},{6,4},{8,10},{10,8},{12,14},{14,12},{16,18},{18,... | collective-permute-start | bytes 1179656 | tf_op jit(solution)/shard_map/ppermute | solution.py:213
  195.0 1.2 copy-start.24
  195.0 13.1 %collective-permute-start.15 = (f32[1,384,256]{2,1,0:T(8,128)}, f32[1,384,256]{2,1,0:T(8,128)S(1)}, u32[]{:S(2)}, u32[]{:S(2)}) collective-permute-start(f32[1,384,256]{2,1,0:T(8,128)} %slice.37), channel_id=1, source_target_pairs={{0,2},{2,0},{4,6},{6,4},{8,10},{10,8},{12,14},{14,12},{16,18},{18,... | collective-permute-start | bytes 1179656 | tf_op jit(solution)/shard_map/ppermute | solution.py:213
  195.6 0.6 copy-start.31
  201.7 0.7 copy-start.25
  201.7 0.9 copy-start.27
  208.1 0.7 copy-start.26
  208.1 0.9 copy-start.28
